TPU v7x, 128 devices: a whole 4x4x4 slice. The times are simulated.
128 devices in a mesh: row: 8 (over z_lo, y), col: 16 (over x, z_hi, core).
Axes of the slice: x: 4, y: 4, z: 4 (z_hi: 2, z_lo: 2; z = z_hi * 2 + z_lo), core: 2. Of those that a mesh axis runs over, the one named last changes fastest.
Arguments:
- film_embeds: float32 [16384, 1024], P(('row', 'col')), may hold values from -120 to 120
- text_embeds: float32 [16384, 1024], P(('col', 'row')), may hold values from -150 to 150
- matched_text_index: int32 [16384], replicated, may hold values from 0 to 16383, as said below
- sharpness_factor: float32 [1], replicated, may hold values from 20 to 60
- affinity_offset: float32 [1], replicated, may hold values from -12 to -6
Outputs:
- clip_loss: float32 [16384], P(('row', 'col'))
- grad_videos: float32 [16384, 1024], P(('row', 'col'))
- grad_captions: float32 [16384, 1024], P(('col', 'row'))
Inputs may be any that keep to these rules, and one draw needn't show every extreme that they name: `matched_text_index`: each caption is the positive of exactly one clip.
All inputs are finite; a program needn't handle non-finite values.
Results may differ from a plain program's by a relative error of at most 0.0037.
Values may be sent and summed in bfloat16 or wider, within the bound.
A program may use at most 128 MiB of HBM per device.

v0:
```python
import math

import jax
import jax.numpy as jnp
from jax import lax
from jax.sharding import PartitionSpec as P


def from_everyone(x, axis):
    peers = lax.axis_size(axis)
    return lax.all_to_all(jnp.broadcast_to(x[None], (peers, *x.shape)), axis, 0, 0, tiled=True)


def laid_out(tiles, dim):
    shape = list(tiles.shape[1:])
    shape[dim] *= tiles.shape[0]
    return jnp.moveaxis(tiles, 0, dim).reshape(shape)


def collect(x, axis, dim):
    tiles = from_everyone(x, axis)
    return laid_out(tiles, dim)


def split_up(x, dim, peers):
    shape = x.shape
    tiles = x.reshape(*shape[:dim], peers, shape[dim] // peers, *shape[dim + 1 :])
    return jnp.moveaxis(tiles, dim, 0)


def sum_at_owner(x, axis, dim):
    peers = lax.axis_size(axis)
    tiles = lax.all_to_all(split_up(x, dim, peers), axis, 0, 0, tiled=True)
    return jnp.sum(tiles, axis=0)


def normalize(embed):
    inverse = lax.rsqrt(jnp.sum(embed * embed, axis=1, keepdims=True) + 1e-06)
    return (embed * inverse, inverse)


def backward_norm(hat, inverse, grad_hat):
    return inverse * (grad_hat - hat * jnp.sum(hat * grad_hat, axis=1, keepdims=True))


def shards(film_embeds, text_embeds, matched_text_index, sharpness_factor, affinity_offset):
    vhat, vnorm = normalize(film_embeds)
    chat, cnorm = normalize(text_embeds)
    width = film_embeds.shape[1]
    vrows = lax.all_gather(vhat.astype(jnp.bfloat16), "col", axis=0, tiled=True)
    crows = collect(chat.astype(jnp.bfloat16), "row", 0)
    film_entries_local = vrows.shape[0]
    caption_row_count = crows.shape[0]
    similarity_multiplier = sharpness_factor[0]
    shift = affinity_offset[0]
    labels = lax.dynamic_slice_in_dim(
        matched_text_index, lax.axis_index("row") * film_entries_local, film_entries_local, 0
    )
    matching_text_indices = lax.axis_index("col") * caption_row_count + jnp.arange(
        caption_row_count, dtype=jnp.int32
    )
    step_rows = math.gcd(film_entries_local, 512)
    vblocks = vrows.reshape(film_entries_local // step_rows, step_rows, width)
    lblocks = labels.reshape(film_entries_local // step_rows, step_rows)

    def tile(pair):
        vblock, lblock = pair
        logits = (
            jnp.dot(vblock, crows.T, preferred_element_type=jnp.float32) * similarity_multiplier
            + shift
        )
        match = lblock[:, None] == matching_text_indices[None, :]
        sign = jnp.where(match, 1.0, -1.0).astype(jnp.float32)
        losses = jnp.sum(jax.nn.softplus(-sign * logits), axis=1)
        coef = (jax.nn.sigmoid(logits) - match.astype(jnp.float32)).astype(jnp.bfloat16)
        return (coef, losses)

    own_rows = film_embeds.shape[0]
    count = own_rows * lax.axis_size("col")
    sub = math.gcd(count, 512)
    vpart = vrows.reshape(count // sub, sub, width)
    lpart = labels.reshape(count // sub, sub)

    def one(pair):
        coef, losses = tile(pair)
        return (
            similarity_multiplier * jnp.dot(coef, crows, preferred_element_type=jnp.float32),
            losses,
        )

    grads, losses = lax.map(one, (vpart, lpart))
    grads, losses = (grads.reshape(count, width), losses.reshape(count))
    filler = jnp.zeros((own_rows * lax.axis_size("col"), 127), jnp.float32)
    both = lax.psum_scatter(
        jnp.concatenate([grads, losses[:, None], filler], axis=1),
        "col",
        scatter_dimension=0,
        tiled=True,
    )
    dvhat = both[:, :width]
    clip_loss = both[:, width]

    def add(total, pair):
        vblock, lblock = pair
        logits = (
            jnp.dot(vblock, crows.T, preferred_element_type=jnp.float32) * similarity_multiplier
            + shift
        )
        match = lblock[:, None] == matching_text_indices[None, :]
        coef = (jax.nn.sigmoid(logits) - match.astype(jnp.float32)).astype(jnp.bfloat16)
        return (
            total
            + lax.dot_general(
                coef, vblock, (((0,), (0,)), ((), ())), preferred_element_type=jnp.float32
            ),
            None,
        )

    total, discarded_value = lax.scan(
        add,
        jnp.zeros((text_embeds.shape[0] * lax.axis_size("row"), width), jnp.float32),
        (vblocks, lblocks),
    )
    dchat = sum_at_owner(similarity_multiplier * total, "row", 0)
    return (clip_loss, backward_norm(vhat, vnorm, dvhat), backward_norm(chat, cnorm, dchat))


def solution(mesh):
    return jax.shard_map(
        shards,
        mesh=mesh,
        in_specs=(P(("row", "col"), None), P(("col", "row"), None), P(), P(), P()),
        out_specs=(P(("row", "col")), P(("row", "col"), None), P(("col", "row"), None)),
        check_vma=False,
    )
```

profile of v0, /device:TPU:0, one launch (start us, length us, event | category | flops | bytes accessed | tf_op | source)
XLA Modules:
  0.0 291.7 jit_solution(14321289743057662920)
XLA Ops:
  7.2 0.0 copy-start
  7.2 0.0 all-gather.2.cloned.1.call-start
  7.2 1.2 multiply_reduce_fusion.3
  8.4 1.8 multiply_convert_fusion.1
  10.3 0.0 all-gather.2.cloned.1.call-update
  10.3 1.2 multiply_reduce_fusion.2
  11.5 0.0 copy-done
  11.5 0.1 multiply_convert_fusion
  11.6 1.6 broadcast_in_dim.42
  13.2 5.9 %all-to-all-start = ((bf16[8,128,1024]{2,1,0:T(8,128)(2,1)}), bf16[8,128,1024]{2,1,0:T(8,128)(2,1)S(1)}, u32[]{:S(2)}, u32[]{:S(2)}) async-start(bf16[8,128,1024]{2,1,0:T(8,128)(2,1)} %broadcast_in_dim.42), calls=%async_computation | async-start | bytes 4194304 | tf_op jit(solution)/shard_map/all_to_all | solution.py:11
  19.1 0.0 reduce-scatter.2.cloned.1.call-start
  19.2 0.7 dynamic_slice.17
  19.9 26.2 %all-to-all-done = bf16[8,128,1024]{2,1,0:T(8,128)(2,1)S(1)} async-done(((bf16[8,128,1024]{2,1,0:T(8,128)(2,1)}), bf16[8,128,1024]{2,1,0:T(8,128)(2,1)S(1)}, u32[]{:S(2)}, u32[]{:S(2)}) %all-to-all-start) | async-done | bytes 2097184 | tf_op jit(solution)/shard_map/all_to_all | solution.py:11
  46.2 39.5 %all-gather.2.cloned.1.call-done = bf16[2048,1024]{1,0:T(8,128)(2,1)} async-done(((bf16[128,1024]{1,0:T(8,128)(2,1)}), bf16[2048,1024]{1,0:T(8,128)(2,1)}) %all-gather.2.cloned.1.call-update) | async-done | bytes 4194320 | tf_op jit(solution)/shard_map/all_gather | solution.py:50
  85.6 37.1 %while.24 = (s32[]{:T(128)}, f32[4,512,1024]{2,1,0:T(8,128)}, f32[4,512]{1,0:T(4,128)S(1)}, f32[]{:T(128)}, bf16[4,512,1024]{2,1,0:T(8,128)(2,1)}, /*index=5*/bf...) while((s32[]{:T(128)}, f32[4,512,1024]{2,1,0:T(8,128)}, ...), condition=%wide.region_4.5_spmd.clone, body=%wide.region_2.4_spmd.clone.sunk | while | flops 2159542784 | bytes 11564665 | solution.py:91
  85.6 5.1 %fusion.47 = (f32[512]{0:T(512)S(1)}, f32[512,1024]{1,0:T(8,128)S(1)}) fusion(s32[1024]{0:T(1024)S(1)} %iota_add_fusion.4, f32[]{:T(128)} %get-tuple-element.319, f32[]{:T(128)} %get-tuple-element.316, s32[512]{0:T(512)S(1)} %bitcast.55, bf16[1024,1024]{1,0:T(8,128)(2,1)S(1)} %get-tuple-element.318, bf16[4,512,1024]{2,1,0:T(8,128)(2,1)} %get-tuple-element.317, ...), kind=kOutput, calls=%fused_computation.9.clone.1 | convolution fusion | flops 1080557056 | bytes 5252608 | tf_op jit(solution)/shard_map/while/body/eval_jaxpr/dot_general | solution.py:69
  90.7 4.1 %bitcast_dynamic-update-slice_fusion.2 = f32[4,512,1024]{2,1,0:T(8,128)} fusion(f32[4,512,1024]{2,1,0:T(8,128)} %get-tuple-element.303, s32[]{:T(128)} %get-tuple-element.302, bf16[1024,1024]{1,0:T(8,128)(2,1)S(1)} %get-tuple-element.318, f32[512,1024]{1,0:T(8,128)S(1)} %get-tuple-element.281, s32[1024]{0:T(1024)S(1)} %iota_add_fusion.4, ...), kind=kOutput, calls=%fused_computation.10.clone.1 | convolution fusion | flops 1078984704 | bytes 6299648 | tf_op jit(solution)/shard_map/while/body/eval_jaxpr/dot_general | solution.py:87
  94.9 5.1 %fusion.47 = (f32[512]{0:T(512)S(1)}, f32[512,1024]{1,0:T(8,128)S(1)}) fusion(s32[1024]{0:T(1024)S(1)} %iota_add_fusion.4, f32[]{:T(128)} %get-tuple-element.319, f32[]{:T(128)} %get-tuple-element.316, s32[512]{0:T(512)S(1)} %bitcast.55, bf16[1024,1024]{1,0:T(8,128)(2,1)S(1)} %get-tuple-element.318, bf16[4,512,1024]{2,1,0:T(8,128)(2,1)} %get-tuple-element.317, ...), kind=kOutput, calls=%fused_computation.9.clone.1 | convolution fusion | flops 1080557056 | bytes 5252608 | tf_op jit(solution)/shard_map/while/body/eval_jaxpr/dot_general | solution.py:69
  100.0 4.2 %bitcast_dynamic-update-slice_fusion.2 = f32[4,512,1024]{2,1,0:T(8,128)} fusion(f32[4,512,1024]{2,1,0:T(8,128)} %get-tuple-element.303, s32[]{:T(128)} %get-tuple-element.302, bf16[1024,1024]{1,0:T(8,128)(2,1)S(1)} %get-tuple-element.318, f32[512,1024]{1,0:T(8,128)S(1)} %get-tuple-element.281, s32[1024]{0:T(1024)S(1)} %iota_add_fusion.4, ...), kind=kOutput, calls=%fused_computation.10.clone.1 | convolution fusion | flops 1078984704 | bytes 6299648 | tf_op jit(solution)/shard_map/while/body/eval_jaxpr/dot_general | solution.py:87
  104.3 5.1 %fusion.47 = (f32[512]{0:T(512)S(1)}, f32[512,1024]{1,0:T(8,128)S(1)}) fusion(s32[1024]{0:T(1024)S(1)} %iota_add_fusion.4, f32[]{:T(128)} %get-tuple-element.319, f32[]{:T(128)} %get-tuple-element.316, s32[512]{0:T(512)S(1)} %bitcast.55, bf16[1024,1024]{1,0:T(8,128)(2,1)S(1)} %get-tuple-element.318, bf16[4,512,1024]{2,1,0:T(8,128)(2,1)} %get-tuple-element.317, ...), kind=kOutput, calls=%fused_computation.9.clone.1 | convolution fusion | flops 1080557056 | bytes 5252608 | tf_op jit(solution)/shard_map/while/body/eval_jaxpr/dot_general | solution.py:69
  109.4 4.0 %bitcast_dynamic-update-slice_fusion.2 = f32[4,512,1024]{2,1,0:T(8,128)} fusion(f32[4,512,1024]{2,1,0:T(8,128)} %get-tuple-element.303, s32[]{:T(128)} %get-tuple-element.302, bf16[1024,1024]{1,0:T(8,128)(2,1)S(1)} %get-tuple-element.318, f32[512,1024]{1,0:T(8,128)S(1)} %get-tuple-element.281, s32[1024]{0:T(1024)S(1)} %iota_add_fusion.4, ...), kind=kOutput, calls=%fused_computation.10.clone.1 | convolution fusion | flops 1078984704 | bytes 6299648 | tf_op jit(solution)/shard_map/while/body/eval_jaxpr/dot_general | solution.py:87
  113.5 5.1 %fusion.47 = (f32[512]{0:T(512)S(1)}, f32[512,1024]{1,0:T(8,128)S(1)}) fusion(s32[1024]{0:T(1024)S(1)} %iota_add_fusion.4, f32[]{:T(128)} %get-tuple-element.319, f32[]{:T(128)} %get-tuple-element.316, s32[512]{0:T(512)S(1)} %bitcast.55, bf16[1024,1024]{1,0:T(8,128)(2,1)S(1)} %get-tuple-element.318, bf16[4,512,1024]{2,1,0:T(8,128)(2,1)} %get-tuple-element.317, ...), kind=kOutput, calls=%fused_computation.9.clone.1 | convolution fusion | flops 1080557056 | bytes 5252608 | tf_op jit(solution)/shard_map/while/body/eval_jaxpr/dot_general | solution.py:69
  118.7 4.1 %bitcast_dynamic-update-slice_fusion.2 = f32[4,512,1024]{2,1,0:T(8,128)} fusion(f32[4,512,1024]{2,1,0:T(8,128)} %get-tuple-element.303, s32[]{:T(128)} %get-tuple-element.302, bf16[1024,1024]{1,0:T(8,128)(2,1)S(1)} %get-tuple-element.318, f32[512,1024]{1,0:T(8,128)S(1)} %get-tuple-element.281, s32[1024]{0:T(1024)S(1)} %iota_add_fusion.4, ...), kind=kOutput, calls=%fused_computation.10.clone.1 | convolution fusion | flops 1078984704 | bytes 6299648 | tf_op jit(solution)/shard_map/while/body/eval_jaxpr/dot_general | solution.py:87
  122.8 0.0 copy-start.2
  122.8 1.3 copy-done.2
  124.1 0.4 copy.10
  124.5 0.1 broadcast_in_dim.43
  124.6 10.3 %concatenate.3 = f32[2048,1152]{1,0:T(8,128)} concatenate(f32[2048,1024]{1,0:T(8,128)} %bitcast.4, f32[2048,1]{1,0:T(8,128)S(1)} %bitcast.52, f32[2048,127]{1,0:T(8,128)S(1)} %broadcast_in_dim.43), dimensions={1} | concatenate | bytes 18874368 | tf_op jit(solution)/shard_map/concatenate | solution.py:95
  134.8 0.0 copy-start.3
  134.8 0.0 reduce-scatter.2.cloned.1.call-update
  135.7 0.8 copy-done.3
  136.5 35.4 %while.25 = (s32[]{:T(128)}, f32[1024,1024]{1,0:T(8,128)}, bf16[4,512,1024]{2,1,0:T(8,128)(2,1)}, bf16[1024,1024]{1,0:T(8,128)(2,1)S(1)}, f32[]{:T(128)}, /*inde...) while((s32[]{:T(128)}, f32[1024,1024]{1,0:T(8,128)}, ...), condition=%wide.region_8.9_spmd.clone, body=%wide.region_7.8_spmd.clone.sunk | while | flops 2154300416 | bytes 12599415 | solution.py:119
  136.5 7.5 %select_add_fusion.2 = f32[1024,1024]{1,0:T(8,128)} fusion(f32[1024,1024]{1,0:T(8,128)} %get-tuple-element.335, pred[]{:T(512)S(6)} %compare.3, bf16[1024,1024]{1,0:T(8,128)(2,1)S(1)} %get-tuple-element.347, s32[1024]{0:T(1024)S(1)} %iota_add_fusion.5, f32[]{:T(128)} %get-tuple-element.349, f32[]{:T(128)} %get-tuple-element.348, ...), kind=kOutput, calls=%fused_computation.24.clone.1 | convolution fusion | flops 2154299392 | bytes 12591105 | tf_op jit(solution)/shard_map/while/body/eval_jaxpr/dot_general | solution.py:113
  144.0 9.4 %select_add_fusion.2 = f32[1024,1024]{1,0:T(8,128)} fusion(f32[1024,1024]{1,0:T(8,128)} %get-tuple-element.335, pred[]{:T(512)S(6)} %compare.3, bf16[1024,1024]{1,0:T(8,128)(2,1)S(1)} %get-tuple-element.347, s32[1024]{0:T(1024)S(1)} %iota_add_fusion.5, f32[]{:T(128)} %get-tuple-element.349, f32[]{:T(128)} %get-tuple-element.348, ...), kind=kOutput, calls=%fused_computation.24.clone.1 | convolution fusion | flops 2154299392 | bytes 12591105 | tf_op jit(solution)/shard_map/while/body/eval_jaxpr/dot_general | solution.py:113
  153.5 9.5 %select_add_fusion.2 = f32[1024,1024]{1,0:T(8,128)} fusion(f32[1024,1024]{1,0:T(8,128)} %get-tuple-element.335, pred[]{:T(512)S(6)} %compare.3, bf16[1024,1024]{1,0:T(8,128)(2,1)S(1)} %get-tuple-element.347, s32[1024]{0:T(1024)S(1)} %iota_add_fusion.5, f32[]{:T(128)} %get-tuple-element.349, f32[]{:T(128)} %get-tuple-element.348, ...), kind=kOutput, calls=%fused_computation.24.clone.1 | convolution fusion | flops 2154299392 | bytes 12591105 | tf_op jit(solution)/shard_map/while/body/eval_jaxpr/dot_general | solution.py:113
  162.9 9.0 %select_add_fusion.2 = f32[1024,1024]{1,0:T(8,128)} fusion(f32[1024,1024]{1,0:T(8,128)} %get-tuple-element.335, pred[]{:T(512)S(6)} %compare.3, bf16[1024,1024]{1,0:T(8,128)(2,1)S(1)} %get-tuple-element.347, s32[1024]{0:T(1024)S(1)} %iota_add_fusion.5, f32[]{:T(128)} %get-tuple-element.349, f32[]{:T(128)} %get-tuple-element.348, ...), kind=kOutput, calls=%fused_computation.24.clone.1 | convolution fusion | flops 2154299392 | bytes 12591105 | tf_op jit(solution)/shard_map/while/body/eval_jaxpr/dot_general | solution.py:113
  171.9 2.6 broadcast_multiply_fusion
  174.5 60.4 %all_to_all.10 = f32[8,128,1024]{2,1,0:T(8,128)} all-to-all(f32[8,128,1024]{2,1,0:T(8,128)S(1)} %bitcast.51), channel_id=1, replica_groups=mesh['row'=8,'col'=16] {'row'}, dimensions={0} | all-to-all | bytes 8388608 | tf_op jit(solution)/shard_map/all_to_all | solution.py:33
  234.9 2.6 reduce_sum.57
  237.5 0.0 copy-start.1
  237.6 0.2 multiply_reduce_fusion
  237.8 1.0 subtract_multiply_fusion
  238.7 41.4 %reduce-scatter.2.cloned.1.call-done = f32[128,1152]{1,0:T(8,128)} async-done(((f32[2048,1152]{1,0:T(8,128)}), f32[128,1152]{1,0:T(8,128)}) %reduce-scatter.2.cloned.1.call-update) | async-done | bytes 589840 | tf_op jit(solution)/shard_map/reduce_scatter | solution.py:94
  280.1 0.0 copy-done.1
  280.2 1.3 multiply_reduce_fusion.1
  281.4 1.5 slice_reduce_fusion
  282.9 2.0 subtract_multiply_fusion.1
  (27 shorter events, 0.3 us)
Async XLA Ops:
  7.2 4.3 %copy-start = (f32[128,1024]{1,0:T(8,128)S(1)}, f32[128,1024]{1,0:T(8,128)}, u32[]{:S(2)}) copy-start(f32[128,1024]{1,0:T(8,128)} %param.10) | copy-start | bytes 1572868
  7.2 78.4 %all-gather.2.cloned.1.call-start = ((), (), s32[]{:S(2)}) async-start(), calls=%async_computation.3 | async-start | bytes 4456448 | tf_op jit(solution)/shard_map/all_gather | solution.py:50
  13.2 32.9 %all-to-all-start = ((bf16[8,128,1024]{2,1,0:T(8,128)(2,1)}), bf16[8,128,1024]{2,1,0:T(8,128)(2,1)S(1)}, u32[]{:S(2)}, u32[]{:S(2)}) async-start(bf16[8,128,1024]{2,1,0:T(8,128)(2,1)} %broadcast_in_dim.42), calls=%async_computation | async-start | bytes 4194304 | tf_op jit(solution)/shard_map/all_to_all | solution.py:11
  19.1 261.0 %reduce-scatter.2.cloned.1.call-start = ((), (), s32[]{:S(2)}) async-start(), calls=%async_computation.4 | async-start | bytes 10027008 | tf_op jit(solution)/shard_map/reduce_scatter | solution.py:94
  122.8 1.4 copy-start.2
  134.8 1.6 copy-start.3
  237.5 42.6 %copy-start.1 = (f32[128,1024]{1,0:T(8,128)S(1)}, f32[128,1024]{1,0:T(8,128)}, u32[]{:S(2)}) copy-start(f32[128,1024]{1,0:T(8,128)} %param.9) | copy-start | bytes 1572868
Sparse Core Ops, SparseCore 0:
  11.0 74.5 all-gather.1
  135.0 145.1 reduce-scatter.1
where the time goes:
time: 293 us; the launch traced here: 292 us
  waiting for transfers between devices  107 us (37%)
  matrix products  72.3 us (25%)
  blocking collectives  60.4 us (21%)
  local copies, waits for them, and re-layouts  16.8 us (6%)
  between operations  14.9 us (5%)
  other arithmetic  14 us (5%)
  starting transfers between devices  5.98 us (2%)
    all_to_all x1, blocking collectives, sum_at_owner(): tiles = lax.all_to_all(split_up(x, dim, peers), axis, 0, 0, tiled=True)  60.4 us
    reduce_scatter x1, waiting for transfers between devices, shards(): lax.psum_scatter(jnp.concatenate([grads, losses[:, None], filler], axis=1...  41.4 us
    all_gather x1, waiting for transfers between devices, shards(): vrows = lax.all_gather(vhat.astype(jnp.bfloat16), 'col', axis=0, tiled=True)  39.5 us
    dot_general x4, matrix products, add(): lax.dot_general(coef, vblock, (((0,), (0,)), ((), ())), preferred_element...  35.4 us
    all_to_all x1, waiting for transfers between devices, from_everyone(): lax.all_to_all(jnp.broadcast_to(x[None], (peers, *x.shape)), axis, 0, 0,...  26.2 us
    dot_general x4, matrix products, tile(): jnp.dot(vblock, crows.T, preferred_element_type=jnp.float32)  20.5 us
    dot_general x4, matrix products, one(): jnp.dot(coef, crows, preferred_element_type=jnp.float32)  16.3 us
    concatenate x1, local copies, waits for them, and re-layouts, shards(): jnp.concatenate([grads, losses[:, None], filler], axis=1)  10.3 us
  transfers between devices with their start and end apart: 3, of which 3 were waited for; matrix products, arithmetic and copies ran while one was open for 16% of the time, Pallas kernels for 0%

commit v1 on v0

v1 whole, which is shorter than its diff:
```python
import functools

import jax
import jax.numpy as jnp
from jax import lax
from jax.experimental import pallas as pl
from jax.experimental.pallas import tpu as pltpu
from jax.sharding import PartitionSpec as P

D = 1024
ROWS = 128
HALF = 64
LOG2E = 1.4426950408889634
LN2 = 0.6931471805599453
MESH = pl.DeviceIdType.MESH
F32 = jnp.float32
BF16 = jnp.bfloat16

RING = (0, 1, 3, 2)
OWN, NEXT, PREV, FAR = 0, 1, 2, 3


def position():
    r, c = lax.axis_index("row"), lax.axis_index("col")
    y, zl = r % 4, r // 4
    core, zh, x = c % 2, (c // 2) % 2, c // 4
    return r, c, x, y, zl, zh, core


def ring_step(i):
    return (i * (i + 1) // 2) % 4


def kernel(
    film, text, labels, scale, shift, loss_out, gv_out, gc_out,
    v16, c16, ct, coef, logits, lab, losses,
    dv_own, dv_sib, dv_tx, dv_core, dv_far, dv_ring, dv_z, dv_ztx,
    dc, dc_tx, dc_far, dc_ring, dc_z,
    ls_core, ls_ring, ls_z, send_sem, recv_sem,
):
    r, c, x, y, zl, zh, core = position()

    def dev(dx=0, dz_hi=0, dcore=0, dy=0, dz_lo=0):
        cc = (((x + dx) % 4) * 2 + (zh + dz_hi) % 2) * 2 + (core + dcore) % 2
        rr = ((zl + dz_lo) % 2) * 4 + (y + dy) % 4
        return (rr, cc)

    x_next, x_prev, x_far = dev(dx=1), dev(dx=3), dev(dx=2)
    y_next, y_prev = dev(dy=1), dev(dy=3)
    z_hi, z_lo, sibling = dev(dz_hi=1), dev(dz_lo=1), dev(dcore=1)

    barrier = pltpu.get_barrier_semaphore()
    peers = (x_next, x_prev, x_far, y_next, y_prev, z_hi, z_lo, sibling)
    for peer in peers:
        pl.semaphore_signal(barrier, inc=1, device_id=peer, device_id_type=MESH)

    copies = []

    def send(src, dst, peer):
        i = len(copies)
        copy = pltpu.make_async_remote_copy(
            src_ref=src, dst_ref=dst, send_sem=send_sem.at[i], recv_sem=recv_sem.at[i],
            device_id=peer, device_id_type=MESH,
        )
        copies.append(copy)
        copy.start()
        return copy

    s = scale[0]
    b = shift[0]

    f = film[...]
    vnorm = lax.rsqrt(jnp.sum(f * f, axis=1, keepdims=True) + 1e-06)
    v16[0:ROWS, :] = (f * vnorm).astype(BF16)
    t = text[...]
    cnorm = lax.rsqrt(jnp.sum(t * t, axis=1, keepdims=True) + 1e-06)
    c16[0:ROWS, :] = (t * cnorm).astype(BF16)

    pl.semaphore_wait(barrier, len(peers))

    def vrow(slot, dk=0, lo=0, n=ROWS):
        return v16.at[pl.ds(slot * 2 * ROWS + dk * ROWS + lo, n), :]

    def crow(slot, lo=0, n=ROWS):
        return c16.at[pl.ds(slot * ROWS + lo, n), :]

    def gather_own(row, z, nxt, prv):
        g = {}
        g["PA"] = send(row(4 * z, lo=0, n=HALF), row(4 * z + PREV, lo=0, n=HALF), nxt)
        g["NA"] = send(row(4 * z, lo=0, n=HALF), row(4 * z + NEXT, lo=0, n=HALF), prv)
        g["PB"] = send(row(4 * z, lo=HALF, n=HALF), row(4 * z + PREV, lo=HALF, n=HALF), nxt)
        g["NB"] = send(row(4 * z, lo=HALF, n=HALF), row(4 * z + NEXT, lo=HALF, n=HALF), prv)
        return g

    def forward_a(row, z, g, nxt):
        g["PA"].wait_recv()
        g["FA"] = send(row(4 * z + PREV, lo=0, n=HALF), row(4 * z + FAR, lo=0, n=HALF), nxt)

    def forward_b(row, z, g, prv):
        g["NB"].wait_recv()
        g["FB"] = send(row(4 * z + NEXT, lo=HALF, n=HALF), row(4 * z + FAR, lo=HALF, n=HALF), prv)

    core_copy = {}

    def to_sibling(slot):
        core_copy[slot] = send(vrow(slot), vrow(slot, dk=1), sibling)

    v_zh = send(vrow(0), vrow(4), z_hi)
    gv0 = gather_own(vrow, 0, x_next, x_prev)
    gc0 = gather_own(crow, 0, y_next, y_prev)
    c_zl = send(crow(0), crow(4), z_lo)
    to_sibling(0)

    for p in range(8):
        dz, i = p // 4, p % 4
        for dk in range(2):
            block = r * 16 + (((x + RING[i]) % 4) * 2 + (zh + dz) % 2) * 2 + (core + dk) % 2
            lab[p, :, dk * ROWS : (dk + 1) * ROWS] = labels[pl.ds(block, 1), :]
    losses[...] = jnp.zeros_like(losses)

    def transpose_c(slot):
        ct[:, slot * ROWS : (slot + 1) * ROWS] = c16[slot * ROWS : (slot + 1) * ROWS, :].T

    scale2 = s * LOG2E
    shift2 = b * LOG2E
    CH = 32

    def act(p, q0, nq):
        logits[0 : nq * ROWS, :] = lax.dot_general(
            c16[q0 * ROWS : (q0 + nq) * ROWS, :], v16[pl.ds(pl.multiple_of(p * 256, 256), 256), :],
            (((1,), (1,)), ((), ())), preferred_element_type=F32,
        )
        ids = lax.broadcasted_iota(jnp.int32, (CH, 256), 0)

        def chunk(j, acc):
            q = q0 + j // (ROWS // CH)
            base = (
                (c * 8 + ((zl + q // 4) % 2) * 4 + (y + ring_step(q % 4)) % 4) * ROWS
                + (j % (ROWS // CH)) * CH
            )
            rows = pl.ds(pl.multiple_of(j * CH, CH), CH)
            match = (lab[p] - base) == ids
            sign = jnp.where(match, -1.0, 1.0).astype(F32)
            e = jnp.exp2((logits[rows, :] * scale2 + shift2) * sign)
            w = 1.0 + e
            inv = pl.reciprocal(w, full_range=False)
            part = jnp.log2(w) * LN2 + (e - (w - 1.0)) * inv
            coef[
                pl.ds(pl.multiple_of(q0 * ROWS + j * CH, CH), CH), pl.ds(pl.multiple_of(p * 256, 256), 256)
            ] = (sign * (e * inv)).astype(BF16)
            for k in range(CH // 8):
                acc = acc + part[k * 8 : (k + 1) * 8, :]
            return acc

        acc = lax.fori_loop(0, nq * (ROWS // CH), chunk, jnp.zeros((8, 256), F32), unroll=2)
        losses[p] = losses[p] + acc[:, 0:ROWS]
        losses[8 + p] = losses[8 + p] + acc[:, ROWS:]

    def act_many(p0, p1, q0, nq):
        def body(p, _):
            act(p, q0, nq)
            return 0

        lax.fori_loop(p0, p1, body, 0)

    transpose_c(0)
    forward_a(vrow, 0, gv0, x_next)
    forward_a(crow, 0, gc0, y_next)
    forward_b(vrow, 0, gv0, x_prev)
    forward_b(crow, 0, gc0, y_prev)
    gv0["NA"].wait_recv()
    to_sibling(NEXT)
    gv0["PB"].wait_recv()
    to_sibling(PREV)
    gc0["NA"].wait_recv()
    gc0["PB"].wait_recv()
    v_zh.wait_recv()
    gv1 = gather_own(vrow, 1, x_next, x_prev)
    to_sibling(4)
    c_zl.wait_recv()
    gc1 = gather_own(crow, 1, y_next, y_prev)
    gv0["FA"].wait_recv()
    gv0["FB"].wait_recv()
    to_sibling(FAR)
    gc0["FA"].wait_recv()
    gc0["FB"].wait_recv()
    for slot in (1, 2, 3, 4):
        transpose_c(slot)
    for slot in (0, 1, 2, 3):
        core_copy[slot].wait_recv()
    act_many(0, 2, 0, 5)
    forward_a(vrow, 1, gv1, x_next)
    forward_a(crow, 1, gc1, y_next)
    forward_b(vrow, 1, gv1, x_prev)
    forward_b(crow, 1, gc1, y_prev)
    act_many(2, 4, 0, 5)
    core_copy[4].wait_recv()
    act_many(4, 5, 0, 5)
    gv1["NA"].wait_recv()
    to_sibling(4 + NEXT)
    gv1["PB"].wait_recv()
    to_sibling(4 + PREV)
    gc1["NA"].wait_recv()
    gc1["PB"].wait_recv()
    transpose_c(5)
    transpose_c(6)
    core_copy[5].wait_recv()
    core_copy[6].wait_recv()
    act_many(0, 5, 5, 2)
    act_many(5, 7, 0, 7)
    gv1["FA"].wait_recv()
    gv1["FB"].wait_recv()
    to_sibling(4 + FAR)
    gc1["FA"].wait_recv()
    gc1["FB"].wait_recv()
    transpose_c(7)
    act_many(0, 7, 7, 1)
    core_copy[7].wait_recv()
    act_many(7, 8, 0, 8)

    ls_copy_core = send(losses.at[pl.ds(8, 8)], ls_core, sibling)

    dv_core_copy = {}

    def make_dv(p):
        for m in range(2):
            rows = slice(m * 512, (m + 1) * 512)
            out = jnp.dot(ct[rows, :], coef[:, p * 256 : (p + 1) * 256], preferred_element_type=F32)
            dv_own[p, rows, :] = out[:, 0:ROWS]
            dv_sib[p, rows, :] = out[:, ROWS:].astype(BF16)
        dv_core_copy[p] = send(dv_sib.at[p], dv_core.at[p], sibling)

    def make_dc(qa, qb):
        left = jnp.concatenate(
            [coef[qa * ROWS : (qa + 1) * ROWS, :], coef[qb * ROWS : (qb + 1) * ROWS, :]], axis=0
        )

        def body(n, _):
            cols = pl.ds(pl.multiple_of(n * 256, 256), 256)
            out = jnp.dot(left, v16[:, cols], preferred_element_type=F32)
            dc[qa, :, cols] = out[0:ROWS]
            dc[qb, :, cols] = out[ROWS:]
            return 0

        lax.fori_loop(0, 4, body, 0)

    dv_far_copy, dv_ring_copy, dc_far_copy, dc_ring_copy = {}, {}, {}, {}

    def dv_send_far(z):
        p = 4 * z + FAR
        dv_core_copy[p].wait_recv()
        dv_tx[p] = (dv_own[p] + dv_core[p].astype(F32)).astype(BF16)
        dv_far_copy[z, 0] = send(dv_tx.at[p, pl.ds(0, 512)], dv_far.at[z, pl.ds(0, 512)], x_next)
        dv_far_copy[z, 1] = send(dv_tx.at[p, pl.ds(512, 512)], dv_far.at[z, pl.ds(512, 512)], x_prev)

    def dv_send_free(z):
        for i, peer, k in ((NEXT, x_next, 1), (PREV, x_prev, 0)):
            p = 4 * z + i
            dv_core_copy[p].wait_recv()
            half = pl.ds(512 * k, 512)
            dv_tx[p, half, :] = (dv_own[p, half, :] + dv_core[p, half, :].astype(F32)).astype(BF16)
            dv_ring_copy[z, i, k] = send(dv_tx.at[p, half], dv_ring.at[2 * z + i - 1, half], peer)

    def dv_send_rest(z):
        for i, peer, k in ((NEXT, x_next, 0), (PREV, x_prev, 1)):
            p = 4 * z + i
            half = pl.ds(512 * k, 512)
            dv_far_copy[z, k].wait_recv()
            dv_tx[p, half, :] = (
                dv_own[p, half, :] + dv_core[p, half, :].astype(F32) + dv_far[z, half, :].astype(F32)
            ).astype(BF16)
            dv_ring_copy[z, i, k] = send(dv_tx.at[p, half], dv_ring.at[2 * z + i - 1, half], peer)

    def dv_total(z):
        p = 4 * z
        dv_core_copy[p].wait_recv()
        for i in (NEXT, PREV):
            for k in range(2):
                dv_ring_copy[z, i, k].wait_recv()
        return (
            dv_own[p] + dv_core[p].astype(F32)
            + (dv_ring[2 * z].astype(F32) + dv_ring[2 * z + 1].astype(F32))
        )

    def dc_send_far(z):
        q = 4 * z + FAR
        dc_tx[q] = dc[q].astype(BF16)
        dc_far_copy[z, 0] = send(dc_tx.at[q, pl.ds(0, HALF)], dc_far.at[z, pl.ds(0, HALF)], y_next)
        dc_far_copy[z, 1] = send(dc_tx.at[q, pl.ds(HALF, HALF)], dc_far.at[z, pl.ds(HALF, HALF)], y_prev)

    def dc_send_free(z):
        for i, peer, k in ((NEXT, y_next, 1), (PREV, y_prev, 0)):
            q = 4 * z + i
            half = pl.ds(HALF * k, HALF)
            dc_tx[q, half, :] = dc[q, half, :].astype(BF16)
            dc_ring_copy[z, i, k] = send(dc_tx.at[q, half], dc_ring.at[2 * z + i - 1, half], peer)

    def dc_send_rest(z):
        for i, peer, k in ((NEXT, y_next, 0), (PREV, y_prev, 1)):
            q = 4 * z + i
            half = pl.ds(HALF * k, HALF)
            dc_far_copy[z, k].wait_recv()
            dc_tx[q, half, :] = (dc[q, half, :] + dc_far[z, half, :].astype(F32)).astype(BF16)
            dc_ring_copy[z, i, k] = send(dc_tx.at[q, half], dc_ring.at[2 * z + i - 1, half], peer)

    def dc_total(z):
        for i in (NEXT, PREV):
            for k in range(2):
                dc_ring_copy[z, i, k].wait_recv()
        return dc[4 * z] + (dc_ring[2 * z].astype(F32) + dc_ring[2 * z + 1].astype(F32))

    make_dv(7)
    make_dv(3)
    make_dc(7, 3)
    dc_send_far(1)
    dc_send_far(0)
    dv_send_far(1)
    dv_send_far(0)
    ls_copy_core.wait_recv()
    for p in range(8):
        losses[p] = losses[p] + ls_core[p]
    ls_copies = []
    for i, peer in ((NEXT, x_next), (PREV, x_prev), (FAR, x_far)):
        for z in range(2):
            ls_copies.append(send(losses.at[4 * z + i], ls_ring.at[3 * z + i - 1], peer))
    make_dv(5)
    make_dv(6)
    make_dc(5, 6)
    dc_send_free(1)
    dv_send_free(1)
    make_dc(1, 2)
    dc_send_rest(1)
    dv_send_rest(1)
    dc_send_free(0)
    make_dv(1)
    make_dv(2)
    dv_send_free(0)
    dc_send_rest(0)
    dv_send_rest(0)
    make_dc(4, 0)
    make_dv(4)
    make_dv(0)
    for copy in ls_copies:
        copy.wait_recv()
    losses[4] = losses[4] + (ls_ring[3] + ls_ring[4] + ls_ring[5])
    losses[0] = losses[0] + (ls_ring[0] + ls_ring[1] + ls_ring[2])
    ls_copy_z = send(losses.at[4], ls_z, z_hi)
    dc_tx[4] = dc_total(1).astype(BF16)
    dc_copy_z = send(dc_tx.at[4], dc_z, z_lo)
    dv_ztx[...] = dv_total(1).astype(BF16)
    dv_copy_z = send(dv_ztx, dv_z, z_hi)

    ls_copy_z.wait_recv()
    loss_out[...] = jnp.sum(losses[0] + ls_z[...], axis=0, keepdims=True)

    total = dc_total(0)
    dc_copy_z.wait_recv()
    dchat = s * (total + dc_z[...].astype(F32))
    chat = text[...] * cnorm
    gc_out[...] = cnorm * (dchat - chat * jnp.sum(chat * dchat, axis=1, keepdims=True))

    total = dv_total(0)
    dv_copy_z.wait_recv()
    dvhat = s * (total + dv_z[...].astype(F32)).T
    vhat = film[...] * vnorm
    gv_out[...] = vnorm * (dvhat - vhat * jnp.sum(vhat * dvhat, axis=1, keepdims=True))

    for copy in copies:
        copy.wait_send()


N_COPIES = 76


def shards(film, text, matched, scale, shift):
    vmem = pl.BlockSpec(memory_space=pltpu.VMEM)
    smem = pl.BlockSpec(memory_space=pltpu.SMEM)
    loss, gv, gc = pl.pallas_call(
        kernel,
        out_shape=(
            jax.ShapeDtypeStruct((1, ROWS), F32),
            jax.ShapeDtypeStruct((ROWS, D), F32),
            jax.ShapeDtypeStruct((ROWS, D), F32),
        ),
        in_specs=[vmem, vmem, vmem, smem, smem],
        out_specs=(vmem, vmem, vmem),
        scratch_shapes=[
            pltpu.VMEM((2048, D), BF16),
            pltpu.VMEM((1024, D), BF16),
            pltpu.VMEM((D, 1024), BF16),
            pltpu.VMEM((1024, 2048), BF16),
            pltpu.VMEM((1024, 256), F32),
            pltpu.VMEM((8, 1, 256), jnp.int32),
            pltpu.VMEM((16, 8, ROWS), F32),
            pltpu.VMEM((8, D, ROWS), F32),
            pltpu.VMEM((8, D, ROWS), BF16),
            pltpu.VMEM((8, D, ROWS), BF16),
            pltpu.VMEM((8, D, ROWS), BF16),
            pltpu.VMEM((2, D, ROWS), BF16),
            pltpu.VMEM((4, D, ROWS), BF16),
            pltpu.VMEM((D, ROWS), BF16),
            pltpu.VMEM((D, ROWS), BF16),
            pltpu.VMEM((8, ROWS, D), F32),
            pltpu.VMEM((8, ROWS, D), BF16),
            pltpu.VMEM((2, ROWS, D), BF16),
            pltpu.VMEM((4, ROWS, D), BF16),
            pltpu.VMEM((ROWS, D), BF16),
            pltpu.VMEM((8, 8, ROWS), F32),
            pltpu.VMEM((6, 8, ROWS), F32),
            pltpu.VMEM((8, ROWS), F32),
            pltpu.SemaphoreType.DMA((N_COPIES,)),
            pltpu.SemaphoreType.DMA((N_COPIES,)),
        ],
        compiler_params=pltpu.CompilerParams(
            collective_id=0, has_side_effects=True, vmem_limit_bytes=60 * 2**20
        ),
        cost_estimate=pl.CostEstimate(flops=13 * 10**9, bytes_accessed=2 * 2**20, transcendentals=0),
    )(film, text, matched.reshape(ROWS, ROWS), scale, shift)
    return loss.reshape(ROWS), gv, gc


def solution(mesh):
    return jax.shard_map(
        shards,
        mesh=mesh,
        in_specs=(P(("row", "col"), None), P(("col", "row"), None), P(), P(), P()),
        out_specs=(P(("row", "col")), P(("row", "col"), None), P(("col", "row"), None)),
        check_vma=False,
    )
```

time: 293 us -> 86.1 us (0.29)
  the two profiles are of different devices: /device:TPU:0 before, /device:TPU:1 now
where the time goes in v1:
time: 86.1 us; the launch traced here: 86 us
  Pallas kernels  80.1 us (93%)
  local copies, waits for them, and re-layouts  3.91 us (5%)
  between operations  1.94 us (2%)
    pallas_call x1, Pallas kernels, shards(): pl.pallas_call(kernel, out_shape=(jax.ShapeDtypeStruct((1, ROWS), F32), j...  80.1 us
    unnamed x7, local copies, waits for them, and re-layouts  3.91 us

profile of v1, /device:TPU:1, one launch (start us, length us, event | category | flops | bytes accessed | tf_op | source)
XLA Modules:
  0.0 86.0 jit_solution(12620257116089356086)
XLA Ops:
  1.9 80.1 %shard_map.76 = (f32[1,128]{1,0:T(1,128)}, f32[128,1024]{1,0:T(8,128)}, f32[128,1024]{1,0:T(8,128)}) custom-call(f32[128,1024]{1,0:T(8,128)} %film.1, f32[128,1024]{1,0:T(8,128)} %text.1, s32[128,128]{1,0:T(8,128)} %bitcast.2, f32[1]{0:T(128)S(6)} %copy.11.scale, f32[1]{0:T(128)S(6)} %copy.12.shift), custom_call_target="tpu_custom_call" | custom-call | flops 12999999488 | bytes 2097152 | tf_op jit(solution)/shard_map/pallas_call | solution.py:378
  82.0 0.0 copy-start.1
  82.1 0.7 copy-done.1
  82.7 0.5 copy.13
  83.2 0.0 copy-start
  83.2 1.9 %copy.14 = f32[128,1024]{1,0:T(8,128)} copy(f32[128,1024]{1,0:T(8,128)} %get-tuple-element.13) | data formatting | bytes 1048576
  85.2 0.0 copy-done
  85.2 0.8 copy.15
Async XLA Ops:
  82.0 0.7 copy-start.1
  83.2 1.9 %copy-start = (f32[128,1024]{1,0:T(8,128)S(1)}, f32[128,1024]{1,0:T(8,128)}, u32[]{:S(2)}) copy-start(f32[128,1024]{1,0:T(8,128)} %get-tuple-element.14) | copy-start | bytes 1572868

commit v2 on v1

--- a/solution.py
+++ b/solution.py
@@ -10,6 +10,7 @@
 D = 1024
 ROWS = 128
 HALF = 64
+CH = 32
 LOG2E = 1.4426950408889634
 LN2 = 0.6931471805599453
 MESH = pl.DeviceIdType.MESH
@@ -27,16 +28,12 @@
     return r, c, x, y, zl, zh, core
 
 
-def ring_step(i):
-    return (i * (i + 1) // 2) % 4
-
-
 def kernel(
-    film, text, labels, scale, shift, loss_out, gv_out, gc_out,
-    v16, c16, ct, coef, logits, lab, losses,
+    film_in, text_in, labels_in, scale_in, shift_in, loss_out, gv_out, gc_out,
+    film, text, labels, scale, shift, gv, gc, v16, c16, ct, coef, logits, lab, base, losses,
     dv_own, dv_sib, dv_tx, dv_core, dv_far, dv_ring, dv_z, dv_ztx,
     dc, dc_tx, dc_far, dc_ring, dc_z,
-    ls_core, ls_ring, ls_z, send_sem, recv_sem,
+    ls_core, ls_ring, ls_z, send_sem, recv_sem, io_sem,
 ):
     r, c, x, y, zl, zh, core = position()
 
@@ -54,7 +51,16 @@
     for peer in peers:
         pl.semaphore_signal(barrier, inc=1, device_id=peer, device_id_type=MESH)
 
-    copies = []
+    loads = [
+        pltpu.make_async_copy(src, dst, io_sem.at[i])
+        for i, (src, dst) in enumerate((
+            (film_in, film), (text_in, text), (labels_in, labels), (scale_in, scale), (shift_in, shift)
+        ))
+    ]
+    for load in loads:
+        load.start()
+
+    copies, sent = [], []
 
     def send(src, dst, peer):
         i = len(copies)
@@ -66,12 +72,11 @@
         copy.start()
         return copy
 
-    s = scale[0]
-    b = shift[0]
-
+    loads[0].wait()
     f = film[...]
     vnorm = lax.rsqrt(jnp.sum(f * f, axis=1, keepdims=True) + 1e-06)
     v16[0:ROWS, :] = (f * vnorm).astype(BF16)
+    loads[1].wait()
     t = text[...]
     cnorm = lax.rsqrt(jnp.sum(t * t, axis=1, keepdims=True) + 1e-06)
     c16[0:ROWS, :] = (t * cnorm).astype(BF16)
@@ -84,19 +89,22 @@
     def crow(slot, lo=0, n=ROWS):
         return c16.at[pl.ds(slot * ROWS + lo, n), :]
 
-    def gather_own(row, z, nxt, prv):
-        g = {}
-        g["PA"] = send(row(4 * z, lo=0, n=HALF), row(4 * z + PREV, lo=0, n=HALF), nxt)
+    def gather_first(row, z, nxt, prv):
+        return {
+            "PA": send(row(4 * z, lo=0, n=HALF), row(4 * z + PREV, lo=0, n=HALF), nxt),
+            "NB": send(row(4 * z, lo=HALF, n=HALF), row(4 * z + NEXT, lo=HALF, n=HALF), prv),
+        }
+
+    def gather_second(row, z, g, nxt, prv):
+        g["PA"].wait_send()
+        g["PB"] = send(row(4 * z, lo=HALF, n=HALF), row(4 * z + PREV, lo=HALF, n=HALF), nxt)
+        g["NB"].wait_send()
         g["NA"] = send(row(4 * z, lo=0, n=HALF), row(4 * z + NEXT, lo=0, n=HALF), prv)
-        g["PB"] = send(row(4 * z, lo=HALF, n=HALF), row(4 * z + PREV, lo=HALF, n=HALF), nxt)
-        g["NB"] = send(row(4 * z, lo=HALF, n=HALF), row(4 * z + NEXT, lo=HALF, n=HALF), prv)
-        return g
-
-    def forward_a(row, z, g, nxt):
+        sent.extend((g["PA"], g["NB"]))
+
+    def forward(row, z, g, nxt, prv):
         g["PA"].wait_recv()
         g["FA"] = send(row(4 * z + PREV, lo=0, n=HALF), row(4 * z + FAR, lo=0, n=HALF), nxt)
-
-    def forward_b(row, z, g, prv):
         g["NB"].wait_recv()
         g["FB"] = send(row(4 * z + NEXT, lo=HALF, n=HALF), row(4 * z + FAR, lo=HALF, n=HALF), prv)
 
@@ -106,16 +114,20 @@
         core_copy[slot] = send(vrow(slot), vrow(slot, dk=1), sibling)
 
     v_zh = send(vrow(0), vrow(4), z_hi)
-    gv0 = gather_own(vrow, 0, x_next, x_prev)
-    gc0 = gather_own(crow, 0, y_next, y_prev)
-    c_zl = send(crow(0), crow(4), z_lo)
+    gv0 = gather_first(vrow, 0, x_next, x_prev)
+    gc0 = gather_first(crow, 0, y_next, y_prev)
     to_sibling(0)
 
+    for load in loads[2:]:
+        load.wait()
+    s = scale[0]
+    b = shift[0]
     for p in range(8):
         dz, i = p // 4, p % 4
         for dk in range(2):
             block = r * 16 + (((x + RING[i]) % 4) * 2 + (zh + dz) % 2) * 2 + (core + dk) % 2
             lab[p, :, dk * ROWS : (dk + 1) * ROWS] = labels[pl.ds(block, 1), :]
+        base[p] = (c * 8 + ((zl + dz) % 2) * 4 + (y + RING[i]) % 4) * ROWS
     losses[...] = jnp.zeros_like(losses)
 
     def transpose_c(slot):
@@ -123,100 +135,106 @@
 
     scale2 = s * LOG2E
     shift2 = b * LOG2E
-    CH = 32
-
-    def act(p, q0, nq):
-        logits[0 : nq * ROWS, :] = lax.dot_general(
-            c16[q0 * ROWS : (q0 + nq) * ROWS, :], v16[pl.ds(pl.multiple_of(p * 256, 256), 256), :],
-            (((1,), (1,)), ((), ())), preferred_element_type=F32,
-        )
+
+    def act_many(p0, p1, q0, nq):
+        left = c16[q0 * ROWS : (q0 + nq) * ROWS, :]
+        for p in range(p0, p1):
+            logits[p, 0 : nq * ROWS, :] = lax.dot_general(
+                left, v16[p * 256 : (p + 1) * 256, :], (((1,), (1,)), ((), ())), preferred_element_type=F32
+            )
         ids = lax.broadcasted_iota(jnp.int32, (CH, 256), 0)
 
-        def chunk(j, acc):
-            q = q0 + j // (ROWS // CH)
-            base = (
-                (c * 8 + ((zl + q // 4) % 2) * 4 + (y + ring_step(q % 4)) % 4) * ROWS
-                + (j % (ROWS // CH)) * CH
-            )
-            rows = pl.ds(pl.multiple_of(j * CH, CH), CH)
-            match = (lab[p] - base) == ids
-            sign = jnp.where(match, -1.0, 1.0).astype(F32)
-            e = jnp.exp2((logits[rows, :] * scale2 + shift2) * sign)
-            w = 1.0 + e
-            inv = pl.reciprocal(w, full_range=False)
-            part = jnp.log2(w) * LN2 + (e - (w - 1.0)) * inv
-            coef[
-                pl.ds(pl.multiple_of(q0 * ROWS + j * CH, CH), CH), pl.ds(pl.multiple_of(p * 256, 256), 256)
-            ] = (sign * (e * inv)).astype(BF16)
-            for k in range(CH // 8):
-                acc = acc + part[k * 8 : (k + 1) * 8, :]
-            return acc
-
-        acc = lax.fori_loop(0, nq * (ROWS // CH), chunk, jnp.zeros((8, 256), F32), unroll=2)
-        losses[p] = losses[p] + acc[:, 0:ROWS]
-        losses[8 + p] = losses[8 + p] + acc[:, ROWS:]
-
-    def act_many(p0, p1, q0, nq):
-        def body(p, _):
-            act(p, q0, nq)
+        def pair(p, _):
+            cols = pl.ds(pl.multiple_of(p * 256, 256), 256)
+
+            def shard(k, acc):
+                mine = lab[p] - base[q0 + k]
+                for j in range(ROWS // CH):
+                    sign = jnp.where((mine - j * CH) == ids, -1.0, 1.0).astype(F32)
+                    rows = pl.ds(pl.multiple_of(k * ROWS + j * CH, CH), CH)
+                    e = jnp.exp2((logits[p, rows, :] * scale2 + shift2) * sign)
+                    w = 1.0 + e
+                    inv = pltpu.reciprocal(w, full_range=False)
+                    part = jnp.log2(w) * LN2 + (e - (w - 1.0)) * inv
+                    coef[pl.ds(pl.multiple_of((q0 + k) * ROWS + j * CH, CH), CH), cols] = (
+                        sign * (e * inv)
+                    ).astype(BF16)
+                    for i in range(CH // 8):
+                        acc = acc + part[i * 8 : (i + 1) * 8, :]
+                return acc
+
+            acc = jnp.zeros((8, 256), F32)
+            acc = shard(0, acc) if nq == 1 else lax.fori_loop(0, nq, shard, acc)
+            losses[p] = losses[p] + acc[:, 0:ROWS]
+            losses[8 + p] = losses[8 + p] + acc[:, ROWS:]
             return 0
 
-        lax.fori_loop(p0, p1, body, 0)
+        lax.fori_loop(p0, p1, pair, 0)
 
     transpose_c(0)
-    forward_a(vrow, 0, gv0, x_next)
-    forward_a(crow, 0, gc0, y_next)
-    forward_b(vrow, 0, gv0, x_prev)
-    forward_b(crow, 0, gc0, y_prev)
+    core_copy[0].wait_recv()
+    act_many(0, 1, 0, 1)
+    gather_second(vrow, 0, gv0, x_next, x_prev)
+    gather_second(crow, 0, gc0, y_next, y_prev)
+    forward(vrow, 0, gv0, x_next, x_prev)
+    forward(crow, 0, gc0, y_next, y_prev)
+    v_zh.wait_send()
+    sent.append(v_zh)
+    c_zl = send(crow(0), crow(4), z_lo)
+    v_zh.wait_recv()
+    gv1 = gather_first(vrow, 1, x_next, x_prev)
+    to_sibling(4)
     gv0["NA"].wait_recv()
     to_sibling(NEXT)
     gv0["PB"].wait_recv()
     to_sibling(PREV)
     gc0["NA"].wait_recv()
     gc0["PB"].wait_recv()
-    v_zh.wait_recv()
-    gv1 = gather_own(vrow, 1, x_next, x_prev)
-    to_sibling(4)
-    c_zl.wait_recv()
-    gc1 = gather_own(crow, 1, y_next, y_prev)
+    transpose_c(1)
+    transpose_c(2)
+    act_many(0, 1, 1, 2)
+    core_copy[1].wait_recv()
+    core_copy[2].wait_recv()
+    act_many(1, 3, 0, 3)
+    gather_second(vrow, 1, gv1, x_next, x_prev)
     gv0["FA"].wait_recv()
     gv0["FB"].wait_recv()
     to_sibling(FAR)
     gc0["FA"].wait_recv()
     gc0["FB"].wait_recv()
-    for slot in (1, 2, 3, 4):
-        transpose_c(slot)
-    for slot in (0, 1, 2, 3):
-        core_copy[slot].wait_recv()
-    act_many(0, 2, 0, 5)
-    forward_a(vrow, 1, gv1, x_next)
-    forward_a(crow, 1, gc1, y_next)
-    forward_b(vrow, 1, gv1, x_prev)
-    forward_b(crow, 1, gc1, y_prev)
-    act_many(2, 4, 0, 5)
+    transpose_c(3)
+    act_many(0, 3, 3, 1)
+    c_zl.wait_recv()
+    gc1 = gather_first(crow, 1, y_next, y_prev)
+    forward(vrow, 1, gv1, x_next, x_prev)
+    core_copy[3].wait_recv()
     core_copy[4].wait_recv()
-    act_many(4, 5, 0, 5)
+    act_many(3, 5, 0, 4)
+    transpose_c(4)
+    act_many(0, 5, 4, 1)
+    gather_second(crow, 1, gc1, y_next, y_prev)
     gv1["NA"].wait_recv()
     to_sibling(4 + NEXT)
     gv1["PB"].wait_recv()
     to_sibling(4 + PREV)
+    forward(crow, 1, gc1, y_next, y_prev)
+    core_copy[5].wait_recv()
+    core_copy[6].wait_recv()
+    act_many(5, 7, 0, 5)
+    gv1["FA"].wait_recv()
+    gv1["FB"].wait_recv()
+    to_sibling(4 + FAR)
     gc1["NA"].wait_recv()
     gc1["PB"].wait_recv()
     transpose_c(5)
     transpose_c(6)
-    core_copy[5].wait_recv()
-    core_copy[6].wait_recv()
-    act_many(0, 5, 5, 2)
-    act_many(5, 7, 0, 7)
-    gv1["FA"].wait_recv()
-    gv1["FB"].wait_recv()
-    to_sibling(4 + FAR)
+    act_many(0, 7, 5, 2)
+    core_copy[7].wait_recv()
+    act_many(7, 8, 0, 7)
     gc1["FA"].wait_recv()
     gc1["FB"].wait_recv()
     transpose_c(7)
-    act_many(0, 7, 7, 1)
-    core_copy[7].wait_recv()
-    act_many(7, 8, 0, 8)
+    act_many(0, 8, 7, 1)
 
     ls_copy_core = send(losses.at[pl.ds(8, 8)], ls_core, sibling)
 
@@ -230,19 +248,15 @@
             dv_sib[p, rows, :] = out[:, ROWS:].astype(BF16)
         dv_core_copy[p] = send(dv_sib.at[p], dv_core.at[p], sibling)
 
-    def make_dc(qa, qb):
-        left = jnp.concatenate(
-            [coef[qa * ROWS : (qa + 1) * ROWS, :], coef[qb * ROWS : (qb + 1) * ROWS, :]], axis=0
-        )
-
+    def make_dc(q):
         def body(n, _):
-            cols = pl.ds(pl.multiple_of(n * 256, 256), 256)
-            out = jnp.dot(left, v16[:, cols], preferred_element_type=F32)
-            dc[qa, :, cols] = out[0:ROWS]
-            dc[qb, :, cols] = out[ROWS:]
+            cols = pl.ds(pl.multiple_of(n * 512, 512), 512)
+            dc[q, :, cols] = jnp.dot(
+                coef[q * ROWS : (q + 1) * ROWS, :], v16[:, cols], preferred_element_type=F32
+            )
             return 0
 
-        lax.fori_loop(0, 4, body, 0)
+        lax.fori_loop(0, 2, body, 0)
 
     dv_far_copy, dv_ring_copy, dc_far_copy, dc_ring_copy = {}, {}, {}, {}
 
@@ -310,12 +324,15 @@
         return dc[4 * z] + (dc_ring[2 * z].astype(F32) + dc_ring[2 * z + 1].astype(F32))
 
     make_dv(7)
-    make_dv(3)
-    make_dc(7, 3)
+    make_dc(7)
     dc_send_far(1)
-    dc_send_far(0)
+    make_dv(5)
     dv_send_far(1)
-    dv_send_far(0)
+    make_dv(6)
+    make_dc(5)
+    make_dc(6)
+    dc_send_free(1)
+    dv_send_free(1)
     ls_copy_core.wait_recv()
     for p in range(8):
         losses[p] = losses[p] + ls_core[p]
@@ -323,33 +340,33 @@
     for i, peer in ((NEXT, x_next), (PREV, x_prev), (FAR, x_far)):
         for z in range(2):
             ls_copies.append(send(losses.at[4 * z + i], ls_ring.at[3 * z + i - 1], peer))
-    make_dv(5)
-    make_dv(6)
-    make_dc(5, 6)
-    dc_send_free(1)
-    dv_send_free(1)
-    make_dc(1, 2)
+    make_dc(4)
+    make_dv(4)
     dc_send_rest(1)
     dv_send_rest(1)
-    dc_send_free(0)
+    make_dc(3)
+    make_dv(3)
+    dc_send_far(0)
+    make_dc(1)
+    make_dc(2)
+    dv_send_far(0)
+    dc_tx[4] = dc_total(1).astype(BF16)
+    dc_copy_z = send(dc_tx.at[4], dc_z, z_lo)
+    dv_ztx[...] = dv_total(1).astype(BF16)
+    dv_copy_z = send(dv_ztx, dv_z, z_hi)
     make_dv(1)
     make_dv(2)
+    dc_send_free(0)
     dv_send_free(0)
     dc_send_rest(0)
     dv_send_rest(0)
-    make_dc(4, 0)
-    make_dv(4)
+    make_dc(0)
     make_dv(0)
     for copy in ls_copies:
         copy.wait_recv()
     losses[4] = losses[4] + (ls_ring[3] + ls_ring[4] + ls_ring[5])
     losses[0] = losses[0] + (ls_ring[0] + ls_ring[1] + ls_ring[2])
     ls_copy_z = send(losses.at[4], ls_z, z_hi)
-    dc_tx[4] = dc_total(1).astype(BF16)
-    dc_copy_z = send(dc_tx.at[4], dc_z, z_lo)
-    dv_ztx[...] = dv_total(1).astype(BF16)
-    dv_copy_z = send(dv_ztx, dv_z, z_hi)
-
     ls_copy_z.wait_recv()
     loss_out[...] = jnp.sum(losses[0] + ls_z[...], axis=0, keepdims=True)
 
@@ -357,24 +374,45 @@
     dc_copy_z.wait_recv()
     dchat = s * (total + dc_z[...].astype(F32))
     chat = text[...] * cnorm
-    gc_out[...] = cnorm * (dchat - chat * jnp.sum(chat * dchat, axis=1, keepdims=True))
+    gc[...] = cnorm * (dchat - chat * jnp.sum(chat * dchat, axis=1, keepdims=True))
+
+    gc_store = pltpu.make_async_copy(gc, gc_out, io_sem.at[0])
+    gc_store.start()
 
     total = dv_total(0)
     dv_copy_z.wait_recv()
     dvhat = s * (total + dv_z[...].astype(F32)).T
     vhat = film[...] * vnorm
-    gv_out[...] = vnorm * (dvhat - vhat * jnp.sum(vhat * dvhat, axis=1, keepdims=True))
-
+    gv[...] = vnorm * (dvhat - vhat * jnp.sum(vhat * dvhat, axis=1, keepdims=True))
+
+    gv_store = pltpu.make_async_copy(gv, gv_out, io_sem.at[1])
+    gv_store.start()
     for copy in copies:
-        copy.wait_send()
+        if not any(copy is other for other in sent):
+            copy.wait_send()
+    gc_store.wait()
+    gv_store.wait()
 
 
 N_COPIES = 76
+
+
+def hand_over(a, b, c, a_out, b_out, c_out, a_held, b_held, c_held, sem):
+    held = (a_held, b_held, c_held)
+    loads = [pltpu.make_async_copy(src, dst, sem.at[0, i]) for i, (src, dst) in enumerate(zip((a, b, c), held))]
+    stores = [pltpu.make_async_copy(src, dst, sem.at[1, i]) for i, (src, dst) in enumerate(zip(held, (a_out, b_out, c_out)))]
+    for load in loads:
+        load.start()
+    for load, store in zip(loads, stores):
+        load.wait()
+        store.start()
+    for store in stores:
+        store.wait()
 
 
 def shards(film, text, matched, scale, shift):
     vmem = pl.BlockSpec(memory_space=pltpu.VMEM)
-    smem = pl.BlockSpec(memory_space=pltpu.SMEM)
+    hbm = pl.BlockSpec(memory_space=pltpu.HBM)
     loss, gv, gc = pl.pallas_call(
         kernel,
         out_shape=(
@@ -382,15 +420,23 @@
             jax.ShapeDtypeStruct((ROWS, D), F32),
             jax.ShapeDtypeStruct((ROWS, D), F32),
         ),
-        in_specs=[vmem, vmem, vmem, smem, smem],
-        out_specs=(vmem, vmem, vmem),
+        in_specs=[hbm] * 5,
+        out_specs=(vmem, hbm, hbm),
         scratch_shapes=[
+            pltpu.VMEM((ROWS, D), F32),
+            pltpu.VMEM((ROWS, D), F32),
+            pltpu.VMEM((ROWS, ROWS), jnp.int32),
+            pltpu.SMEM((1,), F32),
+            pltpu.SMEM((1,), F32),
+            pltpu.VMEM((ROWS, D), F32),
+            pltpu.VMEM((ROWS, D), F32),
             pltpu.VMEM((2048, D), BF16),
             pltpu.VMEM((1024, D), BF16),
             pltpu.VMEM((D, 1024), BF16),
             pltpu.VMEM((1024, 2048), BF16),
-            pltpu.VMEM((1024, 256), F32),
+            pltpu.VMEM((8, 1024, 256), F32),
             pltpu.VMEM((8, 1, 256), jnp.int32),
+            pltpu.SMEM((8,), jnp.int32),
             pltpu.VMEM((16, 8, ROWS), F32),
             pltpu.VMEM((8, D, ROWS), F32),
             pltpu.VMEM((8, D, ROWS), BF16),
@@ -410,12 +456,20 @@
             pltpu.VMEM((8, ROWS), F32),
             pltpu.SemaphoreType.DMA((N_COPIES,)),
             pltpu.SemaphoreType.DMA((N_COPIES,)),
+            pltpu.SemaphoreType.DMA((5,)),
         ],
         compiler_params=pltpu.CompilerParams(
             collective_id=0, has_side_effects=True, vmem_limit_bytes=60 * 2**20
         ),
         cost_estimate=pl.CostEstimate(flops=13 * 10**9, bytes_accessed=2 * 2**20, transcendentals=0),
     )(film, text, matched.reshape(ROWS, ROWS), scale, shift)
+    loss, gv, gc = pl.pallas_call(
+        hand_over,
+        out_shape=tuple(jax.ShapeDtypeStruct(a.shape, a.dtype) for a in (loss, gv, gc)),
+        in_specs=[hbm] * 3,
+        out_specs=(hbm,) * 3,
+        scratch_shapes=[pltpu.VMEM(a.shape, a.dtype) for a in (loss, gv, gc)] + [pltpu.SemaphoreType.DMA((2, 3))],
+    )(loss, gv, gc)
     return loss.reshape(ROWS), gv, gc
 
 

time: 86.1 us -> 69.8 us (0.81)
  the two profiles are of different devices: /device:TPU:1 before, /device:TPU:0 now
where the time goes in v2:
time: 69.8 us; the launch traced here: 69.6 us
  Pallas kernels  67.6 us (97%)
  between operations  2.09 us (3%)
    pallas_call x1, Pallas kernels, shards(): pl.pallas_call(kernel, out_shape=(jax.ShapeDtypeStruct((1, ROWS), F32), j...  65.5 us
    pallas_call x1, Pallas kernels, shards(): pl.pallas_call(hand_over, out_shape=tuple((jax.ShapeDtypeStruct(a.shape,...  2.06 us

profile of v2, /device:TPU:0, one launch (start us, length us, event | category | flops | bytes accessed | tf_op | source)
XLA Modules:
  0.0 69.6 jit_solution(5902939097662058803)
XLA Ops:
  1.9 65.5 %shard_map.76 = (f32[1,128]{1,0:T(1,128)}, f32[128,1024]{1,0:T(8,128)}, f32[128,1024]{1,0:T(8,128)}) custom-call(f32[128,1024]{1,0:T(8,128)} %film_in.1, f32[128,1024]{1,0:T(8,128)} %text_in.1, s32[128,128]{1,0:T(8,128)} %bitcast.2, f32[1]{0:T(128)S(6)} %copy.8.scale_in, f32[1]{0:T(128)S(6)} %copy.9.shift_in), custom_call_target="tpu_custom_call" | custom-call | flops 12999999488 | bytes 2097152 | tf_op jit(solution)/shard_map/pallas_call | solution.py:416
  67.4 2.1 %shard_map.77 = (f32[1,128]{1,0:T(1,128)}, f32[128,1024]{1,0:T(8,128)}, f32[128,1024]{1,0:T(8,128)}) custom-call(f32[1,128]{1,0:T(1,128)} %get-tuple-element.9.a, f32[128,1024]{1,0:T(8,128)} %get-tuple-element.10.b, f32[128,1024]{1,0:T(8,128)} %get-tuple-element.11.c), custom_call_target="tpu_custom_call" | custom-call | tf_op jit(solution)/shard_map/pallas_call | solution.py:466

commit v3 on v2

--- a/solution.py
+++ b/solution.py
@@ -170,6 +170,16 @@
             return 0
 
         lax.fori_loop(p0, p1, pair, 0)
+
+    dv_core_copy = {}
+
+    def make_dv(p):
+        for m in range(2):
+            rows = slice(m * 512, (m + 1) * 512)
+            out = jnp.dot(ct[rows, :], coef[:, p * 256 : (p + 1) * 256], preferred_element_type=F32)
+            dv_own[p, rows, :] = out[:, 0:ROWS]
+            dv_sib[p, rows, :] = out[:, ROWS:].astype(BF16)
+        dv_core_copy[p] = send(dv_sib.at[p], dv_core.at[p], sibling)
 
     transpose_c(0)
     core_copy[0].wait_recv()
@@ -234,19 +244,11 @@
     gc1["FA"].wait_recv()
     gc1["FB"].wait_recv()
     transpose_c(7)
-    act_many(0, 8, 7, 1)
+    act_many(7, 8, 7, 1)
+    make_dv(7)
+    act_many(0, 7, 7, 1)
 
     ls_copy_core = send(losses.at[pl.ds(8, 8)], ls_core, sibling)
-
-    dv_core_copy = {}
-
-    def make_dv(p):
-        for m in range(2):
-            rows = slice(m * 512, (m + 1) * 512)
-            out = jnp.dot(ct[rows, :], coef[:, p * 256 : (p + 1) * 256], preferred_element_type=F32)
-            dv_own[p, rows, :] = out[:, 0:ROWS]
-            dv_sib[p, rows, :] = out[:, ROWS:].astype(BF16)
-        dv_core_copy[p] = send(dv_sib.at[p], dv_core.at[p], sibling)
 
     def make_dc(q):
         def body(n, _):
@@ -323,11 +325,10 @@
                 dc_ring_copy[z, i, k].wait_recv()
         return dc[4 * z] + (dc_ring[2 * z].astype(F32) + dc_ring[2 * z + 1].astype(F32))
 
-    make_dv(7)
+    dv_send_far(1)
     make_dc(7)
     dc_send_far(1)
     make_dv(5)
-    dv_send_far(1)
     make_dv(6)
     make_dc(5)
     make_dc(6)

time: 69.8 us -> 69.1 us (0.990)
  Pallas kernels: 67.6 us -> 66.8 us
    pallas_call x1, Pallas kernels: 65.5 us -> 64.7 us  [shards(): pl.pallas_call(kernel, out_shape=(jax.ShapeDtypeStruct((1, ROWS), F32), j...]
where the time goes in v3:
time: 69.1 us; the launch traced here: 68.9 us
  Pallas kernels  66.8 us (97%)
  between operations  2.09 us (3%)
    pallas_call x1, Pallas kernels, shards(): pl.pallas_call(kernel, out_shape=(jax.ShapeDtypeStruct((1, ROWS), F32), j...  64.7 us
    pallas_call x1, Pallas kernels, shards(): pl.pallas_call(hand_over, out_shape=tuple((jax.ShapeDtypeStruct(a.shape,...  2.06 us

profile of v3, /device:TPU:0, one launch (start us, length us, event | category | flops | bytes accessed | tf_op | source)
XLA Modules:
  0.0 68.9 jit_solution(13811030974085908900)
XLA Ops:
  1.9 64.7 %shard_map.76 = (f32[1,128]{1,0:T(1,128)}, f32[128,1024]{1,0:T(8,128)}, f32[128,1024]{1,0:T(8,128)}) custom-call(f32[128,1024]{1,0:T(8,128)} %film_in.1, f32[128,1024]{1,0:T(8,128)} %text_in.1, s32[128,128]{1,0:T(8,128)} %bitcast.2, f32[1]{0:T(128)S(6)} %copy.8.scale_in, f32[1]{0:T(128)S(6)} %copy.9.shift_in), custom_call_target="tpu_custom_call" | custom-call | flops 12999999488 | bytes 2097152 | tf_op jit(solution)/shard_map/pallas_call | solution.py:417
  66.7 2.1 %shard_map.77 = (f32[1,128]{1,0:T(1,128)}, f32[128,1024]{1,0:T(8,128)}, f32[128,1024]{1,0:T(8,128)}) custom-call(f32[1,128]{1,0:T(1,128)} %get-tuple-element.9.a, f32[128,1024]{1,0:T(8,128)} %get-tuple-element.10.b, f32[128,1024]{1,0:T(8,128)} %get-tuple-element.11.c), custom_call_target="tpu_custom_call" | custom-call | tf_op jit(solution)/shard_map/pallas_call | solution.py:467

commit v4 on v3

--- a/solution.py
+++ b/solution.py
@@ -10,7 +10,7 @@
 D = 1024
 ROWS = 128
 HALF = 64
-CH = 32
+CH = 64
 LOG2E = 1.4426950408889634
 LN2 = 0.6931471805599453
 MESH = pl.DeviceIdType.MESH
@@ -214,19 +214,19 @@
     gc0["FB"].wait_recv()
     transpose_c(3)
     act_many(0, 3, 3, 1)
+    forward(vrow, 1, gv1, x_next, x_prev)
     c_zl.wait_recv()
     gc1 = gather_first(crow, 1, y_next, y_prev)
-    forward(vrow, 1, gv1, x_next, x_prev)
     core_copy[3].wait_recv()
     core_copy[4].wait_recv()
     act_many(3, 5, 0, 4)
-    transpose_c(4)
-    act_many(0, 5, 4, 1)
     gather_second(crow, 1, gc1, y_next, y_prev)
     gv1["NA"].wait_recv()
     to_sibling(4 + NEXT)
     gv1["PB"].wait_recv()
     to_sibling(4 + PREV)
+    transpose_c(4)
+    act_many(0, 5, 4, 1)
     forward(crow, 1, gc1, y_next, y_prev)
     core_copy[5].wait_recv()
     core_copy[6].wait_recv()

time: 69.1 us -> 69.1 us (level)
  no operation moved by 1% of the time
where the time goes in v4:
time: 69.1 us; the launch traced here: 68.9 us
  Pallas kernels  66.9 us (97%)
  between operations  2.09 us (3%)
    pallas_call x1, Pallas kernels, shards(): pl.pallas_call(kernel, out_shape=(jax.ShapeDtypeStruct((1, ROWS), F32), j...  64.8 us
    pallas_call x1, Pallas kernels, shards(): pl.pallas_call(hand_over, out_shape=tuple((jax.ShapeDtypeStruct(a.shape,...  2.06 us

profile of v4, /device:TPU:0, one launch (start us, length us, event | category | flops | bytes accessed | tf_op | source)
XLA Modules:
  0.0 68.9 jit_solution(1840252912353973787)
XLA Ops:
  1.9 64.8 %shard_map.76 = (f32[1,128]{1,0:T(1,128)}, f32[128,1024]{1,0:T(8,128)}, f32[128,1024]{1,0:T(8,128)}) custom-call(f32[128,1024]{1,0:T(8,128)} %film_in.1, f32[128,1024]{1,0:T(8,128)} %text_in.1, s32[128,128]{1,0:T(8,128)} %bitcast.2, f32[1]{0:T(128)S(6)} %copy.8.scale_in, f32[1]{0:T(128)S(6)} %copy.9.shift_in), custom_call_target="tpu_custom_call" | custom-call | flops 12999999488 | bytes 2097152 | tf_op jit(solution)/shard_map/pallas_call | solution.py:417
  66.7 2.1 %shard_map.77 = (f32[1,128]{1,0:T(1,128)}, f32[128,1024]{1,0:T(8,128)}, f32[128,1024]{1,0:T(8,128)}) custom-call(f32[1,128]{1,0:T(1,128)} %get-tuple-element.9.a, f32[128,1024]{1,0:T(8,128)} %get-tuple-element.10.b, f32[128,1024]{1,0:T(8,128)} %get-tuple-element.11.c), custom_call_target="tpu_custom_call" | custom-call | tf_op jit(solution)/shard_map/pallas_call | solution.py:467
